TPU v7x, 32 devices: a whole 2x2x4 slice. The times are simulated.
32 devices in a mesh: seq: 8 (over y, x, core), stream: 4 (over z).
Axes of the slice: x: 2, y: 2, z: 4, core: 2. Of those that a mesh axis runs over, the one named last changes fastest.
Arguments:
- tokens: bfloat16 [4, 1024, 1024], P('stream', 'seq'), may hold values from -6 to 6
- grad_out: bfloat16 [4, 1024, 1024], P('stream', 'seq'), may hold values from -6 to 6
- doc_lengths: int32 [4, 8], P('stream'), may hold values from 1 to 512, 1024 in all within a row
- gain_in: float32 [1024], replicated, may hold values from 0.5 to 1.5
- in_weight: bfloat16 [1024, 6144], replicated, may hold values from -0.1875 to 0.1875
- small_weight: float32 [1024, 24], replicated, may hold values from -0.1875 to 0.1875
- gate_bias: float32 [8], replicated, may hold values from -1 to 1
- decay_rate: float32 [8], replicated, may hold values from 0.0009765625 to 0.1
- conv_weight: float32 [4, 5120], replicated, may hold values from -3 to 3
- gain_head: float32 [128], replicated, may hold values from 0.5 to 1.5
- out_weight: bfloat16 [1024, 1024], replicated, may hold values from -0.1875 to 0.1875
- gain_mid: float32 [1024], replicated, may hold values from 0.5 to 1.5
- gate_up_weight: bfloat16 [1024, 5632], replicated, may hold values from -0.1875 to 0.1875
- down_weight: bfloat16 [2816, 1024], replicated, may hold values from -0.109375 to 0.109375
Outputs:
- output: bfloat16 [4, 1024, 1024], P('stream', 'seq')
- grad_input: float32 [4, 1024, 1024], P('stream', 'seq')
- grad_gain_in: float32 [1024], replicated
- grad_in_weight: float32 [1024, 6144], P(('seq', 'stream'))
- grad_small_weight: float32 [1024, 24], replicated
- grad_gate_bias: float32 [8], replicated
- grad_decay_rate: float32 [8], replicated
- grad_conv_weight: float32 [4, 5120], replicated
- grad_gain_head: float32 [128], replicated
- grad_out_weight: float32 [1024, 1024], P(('seq', 'stream'))
- grad_gain_mid: float32 [1024], replicated
- grad_gate_up_weight: float32 [1024, 5632], P(('seq', 'stream'))
- grad_down_weight: float32 [2816, 1024], P(('seq', 'stream'))
Inputs may be any that keep to these rules, and one draw needn't show every extreme that they name: `doc_lengths`: each row holds the lengths of the 8 consecutive documents of one domain sequence, 1 or more each, summing to 1024; the longest is exactly 512.
All inputs are finite; a program needn't handle non-finite values.
Results may differ from a plain program's by a relative error of at most 0.014.
The roundings to bfloat16 on the way count: a program that leaves them out, or rounds other values in their place, can miss the bound.
Values may be sent and summed in bfloat16 or wider, within the bound.
A program may use at most 256 MiB of HBM per device.

v0:
```python
import functools

import jax
import jax.numpy as jnp
from jax import lax
from jax.experimental import pallas as pl
from jax.experimental.pallas import tpu as pltpu
from jax.sharding import PartitionSpec as P

D = 1024
H = 8
HD = 128
FF = 2816
NH = 2
CONV = 4
GROUPS = 2 + 2 * NH
MIXED = GROUPS - 1
SMALL = NH + 1
DOCS = 8
TILE = 256
EPS = 1e-06

f32 = jnp.float32
bf16 = jnp.bfloat16
MESH = pl.DeviceIdType.MESH
DMA = pltpu.SemaphoreType.DMA
VMEM = pl.BlockSpec(memory_space=pltpu.VMEM)
SMEM = pl.BlockSpec(memory_space=pltpu.SMEM)
ANY = pl.BlockSpec(memory_space=pl.ANY)
LIMIT = 56 * 1024 * 1024
shape = jax.ShapeDtypeStruct


def dot(a, b, dims):
    if isinstance(a, tuple) and isinstance(b, tuple):
        return dot(a[0], b[0], dims) + (dot(a[0], b[1], dims) + dot(a[1], b[0], dims))
    if isinstance(a, tuple):
        return dot(a[0], b, dims) + dot(a[1], b, dims)
    if isinstance(b, tuple):
        return dot(a, b[0], dims) + dot(a, b[1], dims)
    return lax.dot_general(
        a.astype(bf16), b.astype(bf16), ((dims[:1], dims[1:]), ((), ())), preferred_element_type=f32
    )


def nn(a, b):
    return dot(a, b, (1, 0))


def nt(a, b):
    return dot(a, b, (1, 1))


def tn(a, b):
    return dot(a, b, (0, 0))


def halves(x):
    high = x.astype(bf16)
    return high, (x - high.astype(f32)).astype(bf16)


def thirds(x):
    high, low = halves(x)
    return high, low, (x - high.astype(f32) - low.astype(f32)).astype(bf16)


def keep(ref, at, x):
    ref[0, at], ref[1, at] = halves(x)


def kept(ref, at):
    return ref[0, at], ref[1, at]


def nn_exact(ones, x):
    high, low, lowest = thirds(x)
    return nn(ones, high) + (nn(ones, low) + nn(ones, lowest))


def sigmoid(x):
    return 1.0 / (1.0 + jnp.exp(-x))


def softplus(x):
    return jnp.maximum(x, 0.0) + jnp.log(1.0 + jnp.exp(-jnp.abs(x)))


def norm_scale(values):
    return lax.rsqrt(jnp.mean(values * values, axis=-1, keepdims=True) + EPS)


def norm_back(values, scale, gain, grad):
    normal = values * scale
    e = grad * gain
    back = scale * (e - normal * jnp.mean(e * normal, axis=-1, keepdims=True))
    return back, jnp.sum(grad * normal, axis=0, keepdims=True)


def iota(dims, axis):
    return lax.broadcasted_iota(jnp.int32, dims, axis)


def doc_at(starts, positions):
    total = jnp.full(positions.shape, -1, jnp.int32)
    for start in starts:
        total = total + (start <= positions).astype(jnp.int32)
    return total


def doc_starts(lengths_ref):
    starts, at = [], jnp.int32(0)
    for j in range(DOCS):
        starts.append(at)
        at = at + lengths_ref[0, j]
    return starts


def stack2(a, b):
    return jnp.concatenate([a, b], axis=0)


def beside(a, b):
    return jnp.concatenate([a, b], axis=1)


def quad(a, b, c, d):
    return stack2(beside(a, b), beside(c, d))


def rows_of(i, size):
    return pl.ds(pl.multiple_of(i * size, size), size)


def greet(axis, peers):
    barrier = pltpu.get_barrier_semaphore()
    for peer in peers:
        pl.semaphore_signal(barrier, inc=1, device_id={axis: peer}, device_id_type=MESH)
    return lambda: pl.semaphore_wait(barrier, len(peers))


def remote(src, dst, send, receive, axis, peer):
    return pltpu.make_async_remote_copy(src, dst, send, receive, device_id={axis: peer}, device_id_type=MESH)


def flipped(chip, bits, chips):
    total, place = 0, 1
    while place < chips:
        total = total + place * lax.rem(chip // place + bits // place, 2)
        place *= 2
    return total


class Gather:
    def __init__(self, n, T, src, dst, sems):
        self.n, self.T, self.src, self.dst = n, T, src, dst
        self.ss, self.rs, self.fs, self.fr = sems
        self.me = lax.axis_index("seq")
        self.chip, self.side = self.me // 2, lax.rem(self.me, 2)
        self.sib = self.me + 1 - 2 * self.side
        order = sorted(range(1, n // 2), key=lambda k: k.bit_count())
        self.early = [k for k in order if k.bit_count() == 1]
        self.late = [k for k in order if k.bit_count() > 1]

    def at(self, device):
        return self.dst.at[rows_of(device, self.T)]

    def partner(self, k):
        return 2 * flipped(self.chip, k, self.n // 2) + self.side

    def direct(self, k):
        peer = self.sib if k == 0 else self.partner(k)
        return remote(self.src, self.at(self.me), self.ss.at[k], self.rs.at[k], "seq", peer)

    def passed(self, k):
        block = self.at(self.partner(k))
        return remote(block, block, self.fs.at[k], self.fr.at[k], "seq", self.sib)

    def relay(self, k):
        top = 1 << (k.bit_length() - 1)
        for side, last in ((0, top), (1, k & -k)):

            @pl.when(self.side == side)
            def _():
                block = self.at(self.partner(k - last))
                remote(block, block, self.ss.at[k], self.rs.at[k], "seq", self.partner(last)).start()

    def start(self):
        for k in (*self.early, 0):
            self.direct(k).start()

    def pass_on(self, k):
        self.direct(k).wait_recv()
        self.passed(k).start()

    def forward(self):
        for k in self.early:
            self.pass_on(k)
        for k in self.late:
            if k.bit_count() == 2:
                self.relay(k)

    def forward_late(self):
        for k in self.late:
            if k.bit_count() > 2:
                self.relay(k)
            self.pass_on(k)

    def arrive(self):
        self.direct(0).wait_recv()
        for k in range(1, self.n // 2):
            self.passed(k).wait_recv()

    def finish(self):
        for k in range(self.n // 2):
            self.direct(k).wait_send()
            if k:
                self.passed(k).wait_send()


def gather_sems(n):
    return [DMA((n // 2,)) for _ in range(4)]


def conv_of(block, taps, docs, T):
    total = block[8:] * taps[CONV - 1 : CONV]
    for lag in range(1, CONV):
        same = (docs[0] == docs[lag]).astype(f32)
        total = total + block[8 - lag : 8 - lag + T] * (taps[CONV - 1 - lag : CONV - lag] * same)
    return total


def chunk_gates(logits, bias, rate, starts, first, T):
    lane = iota((T, HD), 1)
    shifted = logits + bias
    gate = -rate * softplus(shifted)
    place_i, place_j = iota((T, T), 0), iota((T, T), 1)
    lower = place_j <= place_i
    cumul = nn_exact(lower.astype(bf16), jnp.where(lane == NH, gate, 0.0))
    beta = 2.0 * sigmoid(logits)
    b0, b1 = beta[:, 0:1], beta[:, 1:2]
    g = cumul[:, NH : NH + 1]
    g_row = jnp.transpose(cumul)[NH : NH + 1, :]
    g_last = cumul[T - 1 : T, NH : NH + 1]
    position = first + iota((T, 1), 0)
    docs = [doc_at(starts, position - lag) for lag in range(CONV)]
    doc = docs[0]
    doc_row = doc_at(starts, first + iota((1, T), 1))
    doc_before = doc_at(starts, jnp.full((1, 1), first - 1, jnp.int32))
    doc_last = doc_at(starts, jnp.full((1, 1), first + (T - 1), jnp.int32))
    joined = lower & (doc == doc_row)
    decay = jnp.where(joined, jnp.exp(jnp.where(joined, g - g_row, 0.0)), 0.0)
    strict = jnp.where(place_i == place_j, 0.0, decay)
    from_start = jnp.exp(g) * (doc == doc_before).astype(f32)
    to_end = jnp.exp(jnp.minimum(g_last - g, 0.0)) * (doc == doc_last).astype(f32)
    whole = jnp.exp(g_last) * (doc_last == doc_before).astype(f32)
    return dict(
        shifted=shifted, beta=beta, b=stack2(b0, b1), docs=docs, decay=decay,
        decays=quad(strict, strict, decay, strict), hd=from_start, hd2=stack2(from_start, from_start),
        to_end=stack2(to_end, to_end), whole=whole,
    )


def key_scale(raw):
    return lax.rsqrt(jnp.sum(raw * raw, axis=-1, keepdims=True) + EPS)


def chunk_inputs(block, taps, docs, T):
    conv = conv_of(block, taps, docs, T)
    sig = sigmoid(conv)
    active = conv * sig
    cut = [active[:, i * HD : (i + 1) * HD] for i in range(MIXED)]
    scales = (key_scale(cut[1]), key_scale(cut[2]))
    keys = stack2(cut[1] * scales[0], cut[2] * scales[1])
    values = stack2(cut[3], cut[4])
    return conv, sig, cut[0], keys, values, stack2(*scales)


def inverses(lowers, T):
    size = NH * T
    row, col = iota((size, size), 0), iota((size, size), 1)
    differ = (row & (T - 1)) ^ (col & (T - 1))
    eye = (row == col).astype(f32)
    found = [jnp.where(row == col, 1.0, jnp.where(differ == 0, -a, 0.0)) for a in lowers]
    step = 1
    while step < T:
        level = (differ >= step) & (differ < 2 * step)
        parts = [nn(jnp.where(level, a, 0.0), x) for a, x in zip(lowers, found)]
        found = [x - nn(x, part) for x, part in zip(found, parts)]
        step *= 2
    a_cut = [halves(a) for a in lowers]
    x_cut = [halves(x) for x in found]
    errors = [
        eye - x - (nn(a[0], xc[0]) + (nn(a[0], xc[1]) + nn(a[1], xc[0])))
        for a, x, xc in zip(a_cut, found, x_cut)
    ]
    return [x + nn(xc[0], e) for x, xc, e in zip(found, x_cut, errors)]


def head_gate(mixed, raw):
    scale = norm_scale(mixed)
    return mixed * scale, scale, sigmoid(raw)


def head_taps(taps_ref, head):
    cuts = [taps_ref[:, pl.ds(pl.multiple_of(i * D + head * HD, HD), HD)] for i in range(MIXED)]
    return jnp.concatenate(cuts, axis=1)


def intra_turn(T, starts, bias, rate, taps, small, block_of, invs, ubuf, wbuf, qbuf, pbuf, dbuf, gates, chunks, midway):
    held, lowers = [], []
    for c in chunks:
        first = pl.multiple_of(c * T, T)
        gate = chunk_gates(small[pl.ds(first, T), :], bias, rate, starts, first, T)
        conv, sig, query, keys, values, scales = chunk_inputs(block_of(c), taps, gate["docs"], T)
        key_pair = halves(keys)
        lowers.append(gate["b"] * (nt(key_pair, key_pair) * gate["decays"]))
        held.append((c, gate, query, keys, key_pair, values))
    found = inverses(lowers, T)
    midway()
    for (c, gate, query, keys, key_pair, values), inverse in zip(held, found):
        at, two = rows_of(c, T), rows_of(c, NH * T)
        pair = halves(inverse)
        invs[0, c], invs[1, c] = pair
        both = nn(pair, halves(gate["b"] * beside(values, gate["hd2"] * keys)))
        ubuf[two, :] = both[:, :HD]
        keep(wbuf, two, both[:, HD:])
        query_pair = halves(query)
        qbuf[0, at], qbuf[1, at] = query_pair
        keep(pbuf, at, nt(query_pair, key_pair) * beside(gate["decay"], gate["decay"]))
        keep(dbuf, two, gate["to_end"] * keys)
        gates[at, :] = jnp.where(iota((T, HD), 1) == 0, gate["hd"], gate["whole"])


def across_turn(T, gain, proj, mixed_out, states, news, head_rows, ubuf, wbuf, qbuf, pbuf, dbuf, gates, done, c, state):
    at, two = rows_of(c, T), rows_of(c, NH * T)
    state_pair = halves(state)
    states[0, c], states[1, c] = state_pair
    new = ubuf[two, :] - nn(kept(wbuf, two), state_pair)
    new_pair = halves(new)
    news[0, two], news[1, two] = new_pair
    gate = gates[at, :]
    mixed = gate[:, 0:1] * nn(kept(qbuf, at), state_pair) + nn(kept(pbuf, at), new_pair)
    mixed_out[at, :] = mixed
    raw = proj[at, MIXED * HD :].astype(f32)
    normal, _, sig = head_gate(mixed, raw)
    head_rows[at, :] = ((normal * gain[...]) * (raw * sig)).astype(bf16)
    done(c)
    return gate[0:1, 1:2] * state + tn(kept(dbuf, two), new_pair)


def widened(w_wide, parts):
    w_wide[...] = jnp.zeros((HD, D), bf16)
    for i, part in enumerate(parts):
        w_wide[32 * i : 32 * i + SMALL * H, :] = part


def forward_kernel(
    n, rep, T, lengths, bias_ref, rate_ref, tokens, cotangent, gain_in, w_in, w_small, taps_ref, gain,
    gated, normed_out, out_all, proj_out, small_out, mixed_out, states, news, invs_out, head_rows,
    normed, proj, small, invs, own, tails, w_head, w_wide, tail_rows, xbuf, ubuf, wbuf, qbuf, pbuf, dbuf, gates,
    w_sems, own_sems, o_sems, a_ss, a_rs, t_ss, t_rs, *sems,
):
    me = lax.axis_index("seq")
    head = me // rep
    chips = n // 2
    wait_for_all = greet("seq", [lax.rem(me + k, n) for k in range(1, n)])
    width = MIXED * HD
    loads = [
        pltpu.make_async_copy(
            w_in.at[:, pl.ds(pl.multiple_of(i * D + head * HD, HD), HD)], w_head.at[:, i * HD : (i + 1) * HD], w_sems.at[i]
        )
        for i in range(GROUPS)
    ]
    for load in loads:
        load.start()
    values = tokens[...].astype(f32)
    own[...] = (values * norm_scale(values) * gain_in[...]).astype(bf16)
    local = pltpu.make_async_copy(own, normed.at[rows_of(me, T)], own_sems.at[0])
    local.start()
    wait_for_all()
    first_gather = Gather(n, T, own, normed, sems[:4])
    second_gather = Gather(n, T, cotangent, out_all, sems[4:8])
    keep_out = pltpu.make_async_copy(cotangent, out_all.at[rows_of(me, T)], own_sems.at[2])
    keep_out.start()
    chip, side = first_gather.chip, first_gather.side
    last = own.at[T - 16 : T]

    def tail_copy(k):
        return remote(last, tails.at[chip], t_ss.at[k], t_rs.at[chip], "seq", lax.rem(me + k, n))

    mine = pltpu.make_async_copy(last, tails.at[chip], own_sems.at[1])
    early, late = first_gather.early, first_gather.late

    @pl.when(side == 1)
    def _():
        for k in range(1, n):
            tail_copy(k).start()
        mine.start()

    for k in (0, *early):
        first_gather.direct(k).start()

    starts = doc_starts(lengths)
    bias, rate = bias_ref[head], rate_ref[head]
    taps = head_taps(taps_ref, head)
    widened(w_wide, thirds(jnp.where((iota((SMALL * H, D), 0) & (H - 1)) == head, w_small[...], 0.0)))
    group, lane = iota((HD, HD), 0), iota((HD, HD), 1)
    picks = (((group & 31) >> 3) == lane) & (group < 96) & (lane < SMALL)
    picks = picks.astype(bf16)
    for load in loads:
        load.wait()
    local.wait()

    @pl.when(side == 1)
    def _():
        mine.wait()
        for k in range(1, n):
            tail_copy(k).wait_send()

    for j in range(chips):

        @pl.when(me != 2 * j + 1)
        def _():
            remote(last, tails.at[j], t_ss.at[0], t_rs.at[j], "seq", lax.rem(me + 1, n)).wait_recv()

    found = nn(tails[...].reshape(chips * 16, D), w_head[...]).astype(bf16).astype(f32)
    tail_rows[...] = found[:, :width]
    size = T + 8

    def block_of(c):
        return xbuf[pl.ds(pl.multiple_of(c * size, 8), size), :]

    def project(pair):
        at = rows_of(pair, 2 * T)
        block = normed[at, :]
        result = nn(block, w_head[...]).astype(bf16)
        proj[at, :] = result
        raw = thirds(nt(block, w_wide[...]))
        small[at, :] = nn(raw[0], picks) + (nn(raw[1], picks) + nn(raw[2], picks))
        mixing = result[:, :width].astype(f32)
        before = lax.rem(pair + chips - 1, chips)
        halo = tail_rows[pl.ds(pl.multiple_of(before * 16 + 8, 8), 8), :]
        base = pl.multiple_of(pair * (2 * size), 8)
        xbuf[pl.ds(base, 8), :] = jnp.where(pair > 0, halo, 0.0)
        xbuf[pl.ds(pl.multiple_of(base + 8, 8), T), :] = mixing[:T]
        xbuf[pl.ds(pl.multiple_of(base + size, 8), T + 8), :] = mixing[T - 8 :]

    first_gather.direct(0).wait_recv()
    groups = [(0,)] + [(*ks[i : i + 2],) for ks in (early, late) for i in range(0, len(ks), 2)]
    to_late = (len(early) + 1) // 2

    def midway(g):
        if g == 0:
            first_gather.forward()
        if g == to_late:
            first_gather.forward_late()
            second_gather.start()
        if g == len(groups) - 1:
            second_gather.forward()

    for g, group in enumerate(groups):
        for k in group:
            if k:
                first_gather.passed(k).wait_recv()
        pairs = [flipped(chip, k, chips) for k in group]
        for pair in pairs:
            project(pair)
        intra_turn(
            T, starts, bias, rate, taps, small, block_of, invs, ubuf, wbuf, qbuf, pbuf, dbuf, gates,
            [2 * pair + i for pair in pairs for i in range(2)], functools.partial(midway, g),
        )

    first_gather.finish()
    stores = [
        pltpu.make_async_copy(a, b, o_sems.at[i])
        for i, (a, b) in enumerate(((normed, normed_out), (proj, proj_out), (small, small_out), (invs, invs_out)))
    ]
    for store in stores:
        store.start()
    column = pl.ds(pl.multiple_of(head * HD, HD), HD)

    def row_copy(c):
        return remote(head_rows.at[rows_of(c, T)], gated.at[:, column], a_ss.at[c], a_rs.at[head], "seq", c)

    def send_rows(c):
        @pl.when((c != me) & (lax.rem(me, rep) == 0))
        def _():
            row_copy(c).start()

    across = functools.partial(
        across_turn, T, gain, proj, mixed_out, states, news, head_rows, ubuf, wbuf, qbuf, pbuf, dbuf, gates, send_rows
    )
    lax.fori_loop(0, n, across, jnp.zeros((HD, HD), f32))

    @pl.when(lax.rem(me, rep) == 0)
    def _():
        kept_rows = pltpu.make_async_copy(head_rows.at[rows_of(me, T)], gated.at[:, column], own_sems.at[0])
        kept_rows.start()
        kept_rows.wait()

    keep_out.wait()
    second_gather.forward_late()

    def settle(k, _):
        peer = lax.rem(me + k, n)

        @pl.when(lax.rem(me, rep) == 0)
        def _():
            row_copy(peer).wait_send()

        @pl.when(lax.rem(peer, rep) == 0)
        def _():
            source = peer // rep
            remote(
                head_rows.at[rows_of(me, T)], gated.at[:, pl.ds(pl.multiple_of(source * HD, HD), HD)],
                a_ss.at[peer], a_rs.at[source], "seq", peer,
            ).wait_recv()

        return 0

    lax.fori_loop(1, n, settle, 0)
    second_gather.arrive()
    second_gather.finish()
    for store in stores:
        store.wait()


def forward_scratch(n, T):
    rows = n * T
    return [
        pltpu.VMEM((rows + 8 * n, MIXED * HD), f32), pltpu.VMEM((NH * rows, HD), f32),
        pltpu.VMEM((2, NH * rows, HD), bf16), pltpu.VMEM((2, rows, HD), bf16), pltpu.VMEM((2, rows, NH * T), bf16),
        pltpu.VMEM((2, NH * rows, HD), bf16), pltpu.VMEM((rows, HD), f32),
    ]


def run_forward(n, rep, T, lengths, bias, rate, tokens, cotangent, gain_in, w_in, w_small, taps, gain):
    rows = n * T
    return pl.pallas_call(
        functools.partial(forward_kernel, n, rep, T),
        out_shape=(
            shape((T, D), bf16), shape((rows, D), bf16), shape((rows, D), bf16), shape((rows, GROUPS * HD), bf16),
            shape((rows, HD), f32), shape((rows, HD), f32), shape((2, n, HD, HD), bf16), shape((2, NH * rows, HD), bf16),
            shape((2, n, NH * T, NH * T), bf16), shape((rows, HD), bf16),
        ),
        in_specs=[SMEM] * 3 + [VMEM, VMEM, VMEM, ANY, VMEM, VMEM, VMEM],
        out_specs=[VMEM, ANY, ANY, ANY, ANY, VMEM, VMEM, VMEM, ANY, VMEM],
        scratch_shapes=[
            pltpu.VMEM((rows, D), bf16), pltpu.VMEM((rows, GROUPS * HD), bf16), pltpu.VMEM((rows, HD), f32),
            pltpu.VMEM((2, n, NH * T, NH * T), bf16),
            pltpu.VMEM((T, D), bf16), pltpu.VMEM((n // 2, 16, D), bf16), pltpu.VMEM((D, GROUPS * HD), bf16),
            pltpu.VMEM((HD, D), bf16), pltpu.VMEM((n * 8, MIXED * HD), f32),
            *forward_scratch(n, T),
            DMA((GROUPS,)), DMA((3,)), DMA((4,)), DMA((n,)), DMA((H,)), DMA((n,)), DMA((n // 2,)), *gather_sems(n), *gather_sems(n),
        ],
        compiler_params=pltpu.CompilerParams(vmem_limit_bytes=LIMIT, collective_id=1, has_side_effects=True),
        name="mixer_forward",
    )(lengths, bias, rate, tokens, cotangent, gain_in, w_in, w_small, taps, gain)


def feed_kernel(
    n, T, steps, tokens, gated, cotangent, w_out, gain_mid, w_gate, w_up, w_down,
    result, grad_residual, mid_all, gain_grad, residual, middle, total, grad_mid, own_sem, *sems,
):
    step = pl.program_id(0)
    me = lax.axis_index("seq")
    gather = Gather(n, T, middle, mid_all, sems)
    local = pltpu.make_async_copy(middle, mid_all.at[rows_of(me, T)], own_sem)

    @pl.when(step == 0)
    def _():
        peers = [gather.sib] + [gather.partner(k) for k in range(1, n // 2)]
        wait_for_all = greet("seq", peers)
        found = tokens[...].astype(f32) + nn(gated[...], w_out[...])
        residual[...] = found
        middle[...] = (found * norm_scale(found) * gain_mid[...]).astype(bf16)
        total[...] = found
        grad_mid[...] = jnp.zeros((T, D), f32)
        wait_for_all()
        gather.start()
        local.start()

    gate, up = nn(middle[...], w_gate[...]), nn(middle[...], w_up[...])
    sig = sigmoid(gate)
    silu = gate * sig
    hidden = (silu * up).astype(bf16)
    total[...] += nn(hidden, w_down[...])
    grad_hidden = nt(cotangent[...], w_down[...])
    grad_gate = (grad_hidden * up * (sig * (1.0 + gate * (1.0 - sig)))).astype(bf16)
    grad_up = (grad_hidden * silu).astype(bf16)
    grad_mid[...] += nt(grad_gate, w_gate[...]) + nt(grad_up, w_up[...])

    for at, what in ((5, gather.forward), (8, gather.forward_late)):

        @pl.when(step == at)
        def _():
            what()

    @pl.when(step == steps - 1)
    def _():
        result[...] = total[...].astype(bf16)
        values = residual[...]
        back, gain_part = norm_back(values, norm_scale(values), gain_mid[...], grad_mid[...])
        gain_grad[...] = gain_part
        grad_residual[...] = cotangent[...].astype(f32) + back
        gather.arrive()
        gather.finish()
        local.wait()


def run_feed(n, T, tokens, gated, cotangent, w_out, gain_mid, w_gate_up, w_down):
    steps = FF // TILE
    fixed = lambda *dims: pl.BlockSpec(dims, lambda i: (0, 0))
    return pl.pallas_call(
        functools.partial(feed_kernel, n, T, steps),
        grid=(steps,),
        out_shape=(shape((T, D), bf16), shape((T, D), f32), shape((n * T, D), bf16), shape((1, D), f32)),
        in_specs=[
            fixed(T, D), fixed(T, D), fixed(T, D), fixed(D, D), fixed(1, D),
            pl.BlockSpec((D, TILE), lambda i: (0, i)), pl.BlockSpec((D, TILE), lambda i: (0, i + FF // TILE)),
            pl.BlockSpec((TILE, D), lambda i: (i, 0)),
        ],
        out_specs=[fixed(T, D), fixed(T, D), ANY, fixed(1, D)],
        scratch_shapes=[
            pltpu.VMEM((T, D), f32), pltpu.VMEM((T, D), bf16), pltpu.VMEM((T, D), f32), pltpu.VMEM((T, D), f32),
            DMA, *gather_sems(n),
        ],
        compiler_params=pltpu.CompilerParams(vmem_limit_bytes=LIMIT, collective_id=2, has_side_effects=True),
        name="feed_forward",
    )(tokens, gated, cotangent, w_out, gain_mid, w_gate_up, w_gate_up, w_down)


def backward_turn(
    n, T, head, starts, bias, rate, taps, gain, incoming_of, proj, small, states, fetch,
    gp, grad_small, gconv_w, xbuf, halo, gates_sum, grad_state, done, k, _,
):
    width = MIXED * HD
    lane = iota((T, HD), 1)
    place_i, place_j = iota((T, T), 0), iota((T, T), 1)
    upper = (place_j >= place_i).astype(bf16)
    under = place_j < place_i
    c = n - 1 - k
    first = pl.multiple_of(c * T, T)
    at, two = rows_of(c, T), rows_of(c, NH * T)
    gate = chunk_gates(small[at, :], bias, rate, starts, first, T)
    block = xbuf[pl.ds(first, T + 8), :]
    conv, sig, query, keys, values, scales = chunk_inputs(block, taps, gate["docs"], T)
    key_pair, query_pair = halves(keys), halves(query)
    b, hd, hd2, to_end = gate["b"], gate["hd"], gate["hd2"], gate["to_end"]
    decay2 = beside(gate["decay"], gate["decay"])
    pairs = nt(key_pair, key_pair) * gate["decays"]
    scores = nt(query_pair, key_pair) * decay2
    state = (states[0, c], states[1, c])
    state_grad = grad_state[...]
    new, inverse, mixed = fetch(c)
    raw = proj[at, width:].astype(f32)
    normal, scale, zsig = head_gate(mixed, raw)
    incoming = incoming_of(at)
    passed = incoming * (raw * zsig)
    gates_sum[0:1, :] += jnp.sum(passed * normal, axis=0, keepdims=True)
    grad_z = incoming * (normal * gain[...]) * (zsig * (1.0 + raw * (1.0 - zsig)))
    e = passed * gain[...]
    grad_mixed = scale * (e - normal * jnp.mean(e * normal, axis=-1, keepdims=True))
    gm = halves(grad_mixed)
    ended = halves(to_end * keys)
    grad_pair = halves(state_grad)
    grad_new = tn(halves(scores), gm) + nn(ended, grad_pair)
    grad_right = tn(inverse, halves(grad_new))
    moved = b * grad_right
    grad_state[...] = gate["whole"] * state_grad + tn(halves(hd * query), gm) - tn(halves(hd2 * keys), halves(moved))
    grad_ended = nt(new, grad_pair)
    grad_scores = nt(gm, new)
    grad_lower = jnp.where(gate["decays"] != 0.0, -nt(halves(grad_right), new), 0.0)
    from_grad = nt(gm, state)
    scored = grad_scores * decay2
    grad_query = hd * from_grad + nn(scored, key_pair[0])
    paired = (b * grad_lower) * gate["decays"]
    keyed = nn(key_pair, state)
    grad_keys = (
        tn(scored, query_pair[0]) + to_end * grad_ended - hd2 * nt(moved, state[0])
        + nn(paired, key_pair[0]) + tn(paired, key_pair[0])
    )
    lower_pairs = grad_lower * pairs
    grad_b = jnp.sum(grad_right * (values - hd2 * keyed), axis=-1, keepdims=True) + jnp.sum(
        lower_pairs, axis=-1, keepdims=True
    )
    four = b * lower_pairs
    both = grad_scores * scores
    joint = (four[:T, :T] + four[:T, T:]) + (four[T:, :T] + four[T:, T:]) + (both[:, :T] + both[:, T:])
    crossing = jnp.sum(jnp.where(under, nn_exact(upper, joint), 0.0), axis=-1, keepdims=True)
    start_part = -hd2 * jnp.sum(moved * keyed, axis=-1, keepdims=True)
    start_part = start_part[:T] + start_part[T:] + hd * jnp.sum(query * from_grad, axis=-1, keepdims=True)
    end_part = to_end * jnp.sum(grad_ended * keys, axis=-1, keepdims=True)
    end_part = end_part[:T] + end_part[T:]
    sums_in = jnp.where(lane == 0, start_part, jnp.where(lane == 1, end_part, 0.0))
    after = nn_exact(upper, sums_in)
    before = nn_exact(under.astype(bf16), sums_in)
    whole_part = gate["whole"] * jnp.sum(state_grad * (state[0].astype(f32) + state[1].astype(f32)), keepdims=True)
    grad_gate = crossing + after[:, 0:1] + before[:, 1:2] + whole_part
    shifted = gate["shifted"]
    grad_beta = [grad_b[i * T : (i + 1) * T] * (gate["beta"][:, i : i + 1] * (1.0 - 0.5 * gate["beta"][:, i : i + 1])) for i in range(NH)]
    grad_decay = (-grad_gate * rate * sigmoid(shifted))[:, NH : NH + 1]
    which = lane >> 3
    logit = jnp.where(which == 0, grad_beta[0], jnp.where(which == 1, grad_beta[1], grad_decay))
    grad_logits = jnp.where((lane < SMALL * H) & ((lane & (H - 1)) == head), logit, 0.0)
    gates_sum[1:2, :] += jnp.sum(jnp.where(lane == NH, grad_decay, 0.0), axis=0, keepdims=True)
    gates_sum[2:3, :] += jnp.sum(jnp.where(lane == NH, grad_gate * -softplus(shifted), 0.0), axis=0, keepdims=True)
    high = grad_logits.astype(bf16).astype(f32)
    grad_small[at, :] = (
        high + pltpu.roll(grad_logits - high, 32, 1) + pltpu.roll(high, 64, 1)
    ).astype(bf16)
    projected_out = jnp.sum(keys * grad_keys, axis=-1, keepdims=True)
    grad_raw = (grad_keys - keys * projected_out) * scales
    slope = sig * (1.0 + conv * (1.0 - sig))
    grad_active = jnp.concatenate([grad_query, grad_raw[:T], grad_raw[T:], moved[:T], moved[T:]], axis=1)
    grad_conv = grad_active * slope
    after_block = stack2(grad_conv, halo[...])
    halo[...] = grad_conv[:8]
    position = first + iota((T, 1), 0)
    total = grad_conv * taps[CONV - 1 : CONV]
    taps_grads = [None] * CONV
    taps_grads[CONV - 1] = jnp.sum(grad_conv * block[8:], axis=0, keepdims=True)
    for lag in range(1, CONV):
        same = (doc_at(starts, position + lag) == gate["docs"][0]).astype(f32)
        total = total + after_block[lag : lag + T] * (taps[CONV - 1 - lag : CONV - lag] * same)
        same = (gate["docs"][lag] == gate["docs"][0]).astype(f32)
        taps_grads[CONV - 1 - lag] = jnp.sum(
            grad_conv * (block[8 - lag : 8 - lag + T] * same), axis=0, keepdims=True
        )
    everything = beside(total, grad_z).astype(bf16)
    gp[at, :] = everything
    gconv_w[...] += jnp.concatenate(taps_grads, axis=0)
    done(k)
    return 0


class Chain:
    def __init__(self, own, up_in, down_in, sems, my, m):
        self.own, self.up_in, self.down_in = own, up_in, down_in
        self.us, self.ur, self.ds, self.dr = sems
        self.my, self.m = my, m

    def up(self, q):
        slot = q - self.my
        return self.own(self.my + self.m - 1 - q), self.up_in(slot), slot, self.my + 1, self.us, self.ur

    def down(self, q):
        slot = q - (self.m - 1 - self.my)
        return self.own(self.my - (self.m - 1 - q)), self.down_in(slot), slot, self.my - 1, self.ds, self.dr

    def copy(self, hop):
        own, arrived, slot, peer, send, receive = hop
        return remote(own, arrived, send.at[slot], receive.at[slot], "stream", peer)

    def start(self):
        for q in range(self.m - 1):

            @pl.when(self.my == 0)
            def _():
                self.copy(self.up(q)).start()

            @pl.when(self.my == self.m - 1)
            def _():
                self.copy(self.down(q)).start()

    def tick(self, q):
        for inner, way in (
            ((self.my > 0) & (self.my <= q), self.up),
            ((self.my < self.m - 1) & (self.my >= self.m - 1 - q), self.down),
        ):

            @pl.when(inner)
            def _():
                hop = way(q)
                self.copy(hop).wait_recv()
                own, arrived = hop[:2]

                def add(i, _):
                    own[i] = (own[i].astype(f32) + arrived[i].astype(f32)).astype(bf16)
                    return 0

                if len(own.shape) == 3 and own.shape[0] > 2:
                    lax.fori_loop(0, own.shape[0], add, 0)
                else:
                    own[...] = (own[...].astype(f32) + arrived[...].astype(f32)).astype(bf16)
                self.copy(hop).start()

    def finish(self, write):
        last = self.m - 1

        @pl.when(self.my > 0)
        def _():
            slot = last - self.my
            remote(self.own(self.my), self.up_in(slot), self.us.at[slot], self.ur.at[slot], "stream", self.my - 1).wait_recv()

        @pl.when(self.my < last)
        def _():
            slot = self.my
            remote(self.own(self.my), self.down_in(slot), self.ds.at[slot], self.dr.at[slot], "stream", self.my + 1).wait_recv()

        from_below, from_above = self.up_in(lax.rem(last - self.my, last)), self.down_in(lax.rem(self.my, last))
        found = self.own(self.my)[...].astype(f32) + jnp.where(self.my > 0, from_below[...].astype(f32), 0.0)
        write(found + jnp.where(self.my < last, from_above[...].astype(f32), 0.0))

    def settle(self):
        for q in range(self.m - 1):

            @pl.when(self.my <= q)
            def _():
                self.copy(self.up(q)).wait_send()

            @pl.when(self.my >= self.m - 1 - q)
            def _():
                self.copy(self.down(q)).wait_send()


class Sums:
    def __init__(self, own, arrived, every, sems, me, my, n, m):
        self.own, self.arrived, self.every = own, arrived, every
        self.zs, self.zr, self.ss, self.rs = sems
        self.me, self.my, self.n, self.m = me, my, n, m

    def across(self, k):
        peer = lax.rem(self.my + k, self.m)
        return remote(self.own, self.arrived.at[k - 1], self.zs.at[k - 1], self.zr.at[k - 1], "stream", peer)

    def along(self, k):
        block = self.every.at[self.me]
        return remote(block, block, self.ss.at[k - 1], self.rs.at[k - 1], "seq", lax.rem(self.me + k, self.n))

    def start(self):
        for k in range(1, self.m):
            self.across(k).start()

    def add(self):
        total = self.own[...]
        for k in range(1, self.m):
            self.across(k).wait()
            total = total + self.arrived[k - 1]
        self.every[self.me] = total
        for k in range(1, self.n):
            self.along(k).start()

    def settle(self):
        for k in range(1, self.n):
            self.along(k).wait()


def chain_sems(*lead):
    return [DMA(lead) for _ in range(4)]


def scatter_to(own, arrived, k, send, receive, me, size):
    peer = lax.rem(me + k, size)
    return remote(own.at[peer], arrived.at[me], send.at[k - 1], receive.at[k - 1], "seq", peer)


def back_kernel(
    n, m, rep, T, piece, shard, wide,
    lengths, bias_ref, rate_ref, tokens, grad_residual, gain_in, gain_mid_grad, w_small, taps_ref, gain,
    mid_any, out_any, w_gate_up, w_down, w_out, rows_any, proj_any, small_any, mixed_any, states_any, news_any, invs_any,
    normed_any, w_in_any,
    grad_input, q_w_in, g_out, q_gu_in, g_down, q_sum,
    mid, cot, w_gate, w_up, w_hid, w_head, head_rows, proj, small, mixed, states, news, invs, normed, w_in, w_wide,
    low_all, hidden, grad_gate, grad_up, gp, grad_small, gconv_w, xbuf, halo, gates_sum, grad_state,
    z_gu, z_gu_up, z_gu_down, z_down, z_down_up, z_down_down, z_out, z_out_up, z_out_down, z_w, z_w_up, z_w_down,
    z_sum, z_sum_in, gain_sum, q_gu, q_w, part_own, part_out, part_in, chip_out, chip_in,
    l_sems, i_sems, gu_us, gu_ur, gu_ds, gu_dr, dn_us, dn_ur, dn_ds, dn_dr, ou_us, ou_ur, ou_ds, ou_dr, w_us, w_ur, w_ds, w_dr,
    sum_ss, sum_rs, qgu_ss, qgu_rs, qw_ss, qw_rs, qsum_ss, qsum_rs, p_ss, p_rs, c_ss, c_rs, *sems,
):
    me, my = lax.axis_index("seq"), lax.axis_index("stream")
    head, chip, side = me // rep, me // 2, lax.rem(me, 2)
    sib = me + 1 - 2 * side
    barrier = pltpu.get_barrier_semaphore()
    for k in range(1, n):
        pl.semaphore_signal(barrier, inc=1, device_id={"seq": lax.rem(me + k, n)}, device_id_type=MESH)
    for k in range(1, m):
        pl.semaphore_signal(barrier, inc=1, device_id={"stream": lax.rem(my + k, m)}, device_id_type=MESH)
    first_unit = me * shard
    base = (first_unit // HD - me // (n - 1)) * HD
    offset = first_unit - base
    sources = [
        mid_any, out_any, w_gate_up.at[:, pl.ds(pl.multiple_of(base, HD), wide)],
        w_gate_up.at[:, pl.ds(pl.multiple_of(FF + base, HD), wide)], w_down.at[pl.ds(pl.multiple_of(base, HD), wide)],
        w_out.at[rows_of(head, HD)], rows_any, proj_any, small_any, mixed_any, states_any, news_any, invs_any, normed_any,
    ]
    places = [mid, cot, w_gate, w_up, w_hid, w_head, head_rows, proj, small, mixed, states, news, invs, normed]
    roomy = len(normed.shape) == 2
    loads = [pltpu.make_async_copy(a, b, l_sems.at[i]) for i, (a, b) in enumerate(zip(sources, places)) if i not in (9, 11, 12, 13) or roomy]
    for i in range(GROUPS):
        column = pl.ds(pl.multiple_of(i * D + head * HD, HD), HD)
        loads.append(pltpu.make_async_copy(w_in_any.at[:, column], w_in.at[:, i * HD : (i + 1) * HD], i_sems.at[i]))
    for load in loads[:5]:
        load.start()
    low_all[rows_of(me, T), :] = grad_residual[...].astype(bf16)
    pl.semaphore_wait(barrier, n + m - 2)
    gather = Gather(n, T, low_all.at[rows_of(me, T)], low_all, sems)
    gather.start()

    for load in loads[:5]:
        load.wait()
    for load in loads[5:]:
        load.start()

    def feed_turn(i, _):
        at = rows_of(i, TILE)
        block = mid[at, :]
        gate, up = nn(block, w_gate[...]), nn(block, w_up[...])
        sig = sigmoid(gate)
        silu = gate * sig
        grad_hidden = nt(cot[at, :], w_hid[...])
        own = lambda x: pltpu.roll(x, wide - offset, 1)[:, :shard].astype(bf16)
        hidden[at, :] = own(silu * up)
        grad_gate[at, :] = own(grad_hidden * up * (sig * (1.0 + gate * (1.0 - sig))))
        grad_up[at, :] = own(grad_hidden * silu)
        return 0

    lax.fori_loop(0, n * T // TILE, feed_turn, 0)
    downs = Chain(lambda d: z_down.at[d], lambda i: z_down_up.at[i], lambda i: z_down_down.at[i], (dn_us, dn_ur, dn_ds, dn_dr), my, m)
    ups = [
        Chain(
            lambda d, j=j: z_gu.at[j, d], lambda i, j=j: z_gu_up.at[j, i], lambda i, j=j: z_gu_down.at[j, i],
            (gu_us.at[j], gu_ur.at[j], gu_ds.at[j], gu_dr.at[j]), my, m,
        )
        for j in range(2)
    ]
    part = tn(hidden[...], cot[...])
    for d in range(m):
        z_down[d] = part[d * (shard // m) : (d + 1) * (shard // m)].astype(bf16)
    downs.start()
    gather.forward()
    for j, grads in enumerate((grad_gate, grad_up)):
        if j:
            gather.forward_late()

        def strip_turn(t, _, j=j, grads=grads):
            found = tn(mid[:, rows_of(t, TILE)], grads[...])
            for i in range(TILE // piece):
                z_gu[j, i % m, t * (TILE // piece // m) + i // m] = found[i * piece : (i + 1) * piece].astype(bf16)
            return 0

        lax.fori_loop(0, D // TILE, strip_turn, 0)
        ups[j].start()
    w_high, w_low = halves(w_small[...])
    widened(w_wide, (w_high, w_high, w_low))
    gather.arrive()
    gather.finish()
    for load in loads[5:]:
        load.wait()
    rows = tn(head_rows[...], low_all[...])
    for share in range(rep):

        @pl.when(lax.rem(me, rep) == share)
        def _():
            for d in range(m):
                at = share * (HD // rep) + d * piece
                z_out[d] = rows[at : at + piece].astype(bf16)

    outs = Chain(lambda d: z_out.at[d], lambda i: z_out_up.at[i], lambda i: z_out_down.at[i], (ou_us, ou_ur, ou_ds, ou_dr), my, m)
    outs.start()
    if not roomy:
        normed = mid
        late = pltpu.make_async_copy(normed_any, normed, l_sems.at[13])
        late.start()
        late.wait()

    width = MIXED * HD
    starts = doc_starts(lengths)
    bias, rate = bias_ref[head], rate_ref[head]
    taps = head_taps(taps_ref, head)
    xbuf[0:8, :] = jnp.zeros((8, width), f32)
    halo[...] = jnp.zeros((8, width), f32)
    gconv_w[...] = jnp.zeros(gconv_w.shape, f32)
    gates_sum[...] = jnp.zeros((8, HD), f32)
    grad_state[...] = jnp.zeros((HD, HD), f32)

    def fill(c, _):
        xbuf[pl.ds(pl.multiple_of(8 + c * T, 8), T), :] = proj[rows_of(c, T), :width].astype(f32)
        return 0

    lax.fori_loop(0, n, fill, 0)

    def normed_rows(at):
        if roomy:
            return normed[at, :].astype(f32)
        return mid[at, :].astype(f32)

    gain_sum[...] = jnp.zeros((1, D), f32)

    def sibling_copy(j):
        return remote(part_out.at[j], part_in.at[j], p_ss.at[j], p_rs.at[j], "seq", sib)

    def owner_copy(j):
        return remote(chip_out.at[j], chip_in.at[chip], c_ss.at[j], c_rs.at[chip], "seq", 2 * j + side)

    def form(j):
        at = rows_of(j, 2 * T)
        found = nt(gp[at, :], w_in[...]) + nn(grad_small[at, :], w_wide[...])
        if rep > 1:
            found = found * (lax.rem(me, rep) == 0).astype(f32)
        gain_sum[...] += jnp.sum(found * normed_rows(at), axis=0, keepdims=True)
        for i in range(2):

            @pl.when(side == i)
            def _():
                part_own[j] = found[i * T : (i + 1) * T].astype(part_own.dtype)
                part_out[j] = found[(1 - i) * T : (2 - i) * T].astype(bf16)

        sibling_copy(j).start()

    def join(j):
        sibling_copy(j).wait_recv()
        found = part_own[j].astype(f32) + part_in[j].astype(f32)
        part_own[j] = found.astype(part_own.dtype)
        chip_out[j] = found.astype(bf16)

        @pl.when(chip != j)
        def _():
            owner_copy(j).start()

    hops = [(chain, q) for chain in (downs, *ups) for q in range(1, m - 1)]

    def after_turn(k):
        c = n - 1 - k

        @pl.when(lax.rem(k, 2) == 1)
        def _():
            form(c // 2)

        @pl.when((lax.rem(k, 2) == 0) & (k > 0))
        def _():
            join((c + 1) // 2)

        for i, (chain, q) in enumerate(hops):

            @pl.when(k == 3 * i // 2)
            def _():
                chain.tick(q)

    def fetch(c):
        if roomy:
            return kept(news, rows_of(c, NH * T)), (invs[0, c], invs[1, c]), mixed[rows_of(c, T), :]
        late = [
            pltpu.make_async_copy(news_any.at[:, rows_of(c, NH * T)], news, l_sems.at[11]),
            pltpu.make_async_copy(invs_any.at[:, pl.ds(c, 1)], invs, l_sems.at[12]),
            pltpu.make_async_copy(mixed_any.at[rows_of(c, T)], mixed, l_sems.at[9]),
        ]
        for load in late:
            load.start()
        for load in late:
            load.wait()
        return (news[0], news[1]), (invs[0, 0], invs[1, 0]), mixed[...]

    turn = functools.partial(
        backward_turn, n, T, head, starts, bias, rate, taps, gain, lambda at: nt(low_all[at, :], w_head[...]),
        proj, small, states, fetch, gp, grad_small, gconv_w, xbuf, halo, gates_sum, grad_state, after_turn,
    )
    lax.fori_loop(0, n, turn, 0)

    small_t = tn(grad_small[...], normed[...])
    small_t = small_t[: SMALL * H] + small_t[32 : 32 + SMALL * H]
    z_sum[0:1, :] = gain_mid_grad[...]
    for i in range(SMALL):
        z_sum[1 + i : 2 + i, :] = jnp.sum(small_t[i * H : (i + 1) * H], axis=0, keepdims=True)
    z_sum[4:8, :width] = gconv_w[...]
    for i in range(3):
        z_sum[4 + i : 5 + i, width : width + HD] = gates_sum[i : i + 1, :]
    z_sum[7:8, width : width + HD] = jnp.zeros((1, HD), f32)
    gain_part = gain_sum[...] / gain_in[...]
    cut = D - width - HD
    for i in range(4):
        z_sum[4 + i : 5 + i, width + HD :] = gain_part[:, i * cut : (i + 1) * cut]
    first_sums = Sums(z_sum, z_sum_in, q_sum, (sum_ss, sum_rs, qsum_ss, qsum_rs), me, my, n, m)
    first_sums.start()

    lines = D // TILE
    units, strip = n // lines, piece * m

    def line(i):
        return Chain(
            lambda d: z_w.at[i, d], lambda j: z_w_up.at[i, j], lambda j: z_w_down.at[i, j],
            (w_us.at[i], w_ur.at[i], w_ds.at[i], w_dr.at[i]), my, m,
        )

    def line_turn(i, _):
        cuts = []
        for u in range(units):
            first = (i + u * lines) * strip
            if strip % HD == 0:
                first = pl.multiple_of(first, HD)
            cuts.append(normed[:, pl.ds(first, strip)])
        found = tn(jnp.concatenate(cuts, axis=1), gp[...])
        for u in range(units):
            for d in range(m):
                at = u * strip + d * piece
                z_w[i, d, u] = found[at : at + piece].astype(bf16)
        line(i).start()
        return 0

    if strip % HD == 0:
        line_turn(0, 0)
        join(0)
        lax.fori_loop(1, lines, line_turn, 0)
    else:
        for i in range(lines):
            line_turn(i, 0)
        join(0)
    ins = [line(i) for i in range(lines)]
    for i, (chain, q) in enumerate(hops):
        if 3 * i // 2 >= n:
            chain.tick(q)

    def write_down(x):
        g_down[...] = x

    def write_out(x):
        g_out[...] = x

    downs.finish(write_down)
    for j in range(2):

        def write_up(x, j=j):
            q_gu[:, j] = x.astype(bf16)

        ups[j].finish(write_up)
    q_ups = [scatter_to(q_gu, q_gu_in, k, qgu_ss, qgu_rs, me, n) for k in range(1, n)]
    for copy in q_ups:
        copy.start()
    q_gu_in[me] = q_gu[me]
    for q in range(1, m - 1):
        outs.tick(q)

    def input_gradient():
        total = part_own[chip].astype(f32)
        for k in range(1, n // 2):
            other = lax.rem(chip + k, n // 2)
            remote(chip_out.at[other], chip_in.at[other], c_ss.at[other], c_rs.at[other], "seq", 2 * other + side).wait_recv()
            total = total + chip_in[other].astype(f32)
        values = tokens[...].astype(f32)
        part, _ = norm_back(values, norm_scale(values), gain_in[...], total)
        grad_input[...] = grad_residual[...] + part

    def deliver(i):
        def write_in(x):
            for u in range(units):
                q_w[i + u * lines] = x[u].astype(bf16)

        ins[i].finish(write_in)
        for j in range(i, n, lines):

            @pl.when(me != j)
            def _():
                remote(q_w.at[j], q_w_in.at[me], qw_ss.at[j], qw_rs.at[me], "seq", j).start()

    first_sums.add()
    for i, chain in enumerate(ins):
        for q in range(1, m - 1):
            chain.tick(q)
        if i:
            deliver(i - 1)
        if i == 1:
            outs.finish(write_out)
        if i == 2:
            input_gradient()
    deliver(len(ins) - 1)
    q_w_in[me] = q_w[me]
    for chain in (downs, *ups, outs, *ins):
        chain.settle()

    def settle(j, _):
        sibling_copy(j).wait_send()

        @pl.when(chip != j)
        def _():
            owner_copy(j).wait_send()

        return 0

    lax.fori_loop(0, n // 2, settle, 0)
    first_sums.settle()
    for copy in q_ups:
        copy.wait()
    for k in range(1, n):
        peer = lax.rem(me + k, n)
        remote(q_w.at[peer], q_w_in.at[me], qw_ss.at[peer], qw_rs.at[me], "seq", peer).wait_send()
        remote(q_w.at[peer], q_w_in.at[peer], qw_ss.at[peer], qw_rs.at[peer], "seq", peer).wait_recv()


def run_back(n, m, rep, T, lengths, bias, rate, tokens, grad_residual, gain_in, gain_mid_grad, w_small, taps, gain,
             mid, cot, w_gate_up, w_down, w_out, head_rows, proj, small, mixed, states, news, invs, normed, w_in):
    rows, piece, shard = n * T, D // (n * m), FF // n
    wide = -(-(shard + HD - 1) // HD) * HD
    vm, roomy = pltpu.VMEM, rows <= 1024
    band = GROUPS * HD

    def chained(*dims, lead=()):
        return [vm((*lead, m, *dims), bf16), vm((*lead, m - 1, *dims), bf16), vm((*lead, m - 1, *dims), bf16)]

    return pl.pallas_call(
        functools.partial(back_kernel, n, m, rep, T, piece, shard, wide),
        out_shape=(
            shape((T, D), f32), shape((n, piece, band), bf16), shape((piece, D), f32), shape((n, 2, piece, shard), bf16),
            shape((shard // m, D), f32), shape((n, 8, D), f32),
        ),
        in_specs=[SMEM] * 3 + [VMEM] * 7 + [ANY] * 14,
        out_specs=[VMEM] * 6,
        scratch_shapes=[
            vm((rows, D), bf16), vm((rows, D), bf16), vm((D, wide), bf16), vm((D, wide), bf16), vm((wide, D), bf16),
            vm((HD, D), bf16), vm((rows, HD), bf16), vm((rows, band), bf16), vm((rows, HD), f32), vm((rows if roomy else T, HD), f32),
            vm((2, n, HD, HD), bf16), vm((2, NH * (rows if roomy else T), HD), bf16), vm((2, n if roomy else 1, NH * T, NH * T), bf16),
            vm((rows, D) if roomy else (1, 16, HD), bf16), vm((D, band), bf16), vm((HD, D), bf16),
            vm((rows, D), bf16), vm((rows, shard), bf16), vm((rows, shard), bf16), vm((rows, shard), bf16),
            vm((rows, band), bf16), vm((rows, HD), bf16), vm((CONV, MIXED * HD), f32), vm((rows + 8, MIXED * HD), f32),
            vm((8, MIXED * HD), f32), vm((8, HD), f32), vm((HD, HD), f32),
            *chained(n, piece, shard, lead=(2,)), *chained(shard // m, D), *chained(piece, D), *chained(n * TILE // D, piece, band, lead=(D // TILE,)),
            vm((8, D), f32), vm((m - 1, 8, D), f32), vm((1, D), f32), vm((n, 2, piece, shard), bf16), vm((n, piece, band), bf16),
            vm((n // 2, T, D), f32 if roomy else bf16), *[vm((n // 2, T, D), bf16)] * 4,
            DMA((14,)), DMA((GROUPS,)), *chain_sems(2, m - 1), *chain_sems(m - 1), *chain_sems(m - 1),
            *chain_sems(D // TILE, m - 1), DMA((m - 1,)), DMA((m - 1,)), DMA((n - 1,)), DMA((n - 1,)), DMA((n,)), DMA((n,)),
            DMA((n - 1,)), DMA((n - 1,)),
            *[DMA((n // 2,))] * 4, *gather_sems(n),
        ],
        compiler_params=pltpu.CompilerParams(vmem_limit_bytes=(60 if roomy else 63) * 1024 * 1024, collective_id=3, has_side_effects=True),
        name="backward",
    )(lengths, bias, rate, tokens, grad_residual, gain_in, gain_mid_grad, w_small, taps, gain,
      mid, cot, w_gate_up, w_down, w_out, head_rows, proj, small, mixed, states, news, invs, normed, w_in)


def output_kernel(
    n, rep, shard, result_in, grad_input_in, w_parts, out_part, gu_parts, down_part, sums,
    result, grad_input, g_in, g_out, g_gate_up, g_down, g_gain_in, g_gain_mid, g_small, g_bias, g_rate, g_taps, g_gain_head,
):
    result[...] = result_in[...]
    grad_input[...] = grad_input_in[...]
    g_out[...] = out_part[...]
    g_down[...] = down_part[...]
    for i in range(2):
        for source in range(n):
            at = i * FF + source * shard
            g_gate_up[:, at : at + shard] = gu_parts[source, i].astype(f32)
    g_gain_mid[...] = jnp.sum(sums[:, 0:1, :], axis=0)
    width = MIXED * HD
    cut = D - width - HD
    for i in range(4):
        g_gain_in[:, i * cut : (i + 1) * cut] = jnp.sum(sums[:, 4 + i : 5 + i, width + HD :], axis=0)
    gain_total = jnp.zeros((1, HD), f32)
    for h in range(H):
        found = sums[h * rep]
        part = w_parts[h * rep].astype(f32)
        for j in range(SMALL):
            g_small[j * H + h : j * H + h + 1, :] = found[1 + j : 2 + j, :]
        for i in range(MIXED):
            g_taps[:, i * D + h * HD : i * D + (h + 1) * HD] = found[4 : 4 + CONV, i * HD : (i + 1) * HD]
        for i in range(GROUPS):
            g_in[:, i * D + h * HD : i * D + (h + 1) * HD] = part[:, i * HD : (i + 1) * HD]
        gain_total = gain_total + found[4:5, width : width + HD]
        g_bias[h] = found[5, width + NH]
        g_rate[h] = found[6, width + NH]
    g_gain_head[...] = gain_total


def run_output(n, rep, *parts):
    result, grad_input, w_parts, out_part, gu_parts, down_part, sums = parts
    piece, shard = out_part.shape[0], gu_parts.shape[-1]
    return pl.pallas_call(
        functools.partial(output_kernel, n, rep, shard),
        out_shape=(
            shape(result.shape, bf16), shape(grad_input.shape, f32), shape((piece, GROUPS * D), f32), shape((piece, D), f32),
            shape((piece, 2 * FF), f32), shape(down_part.shape, f32), shape((1, D), f32), shape((1, D), f32),
            shape((SMALL * H, D), f32), shape((H,), f32), shape((H,), f32), shape((CONV, MIXED * D), f32), shape((1, HD), f32),
        ),
        in_specs=[VMEM] * 7,
        out_specs=[VMEM] * 9 + [SMEM] * 2 + [VMEM] * 2,
        compiler_params=pltpu.CompilerParams(vmem_limit_bytes=LIMIT),
        name="outputs",
    )(*parts)


def on_device(tokens, grad_out, doc_lengths, gain_in, in_weight, small_weight, gate_bias, decay_rate, conv_weight,
              gain_head, out_weight, gain_mid, gate_up_weight, down_weight):
    seq, stream = lax.axis_size("seq"), lax.axis_size("stream")
    rep = seq // H
    T = tokens.shape[1]
    gain = gain_head.reshape(1, HD)
    gain_in, gain_mid = gain_in.reshape(1, D), gain_mid.reshape(1, D)
    rows, cotangent, small_weight = tokens[0], grad_out[0], small_weight.T
    gated, normed, out_all, proj, small, mixed, states, news, invs, head_rows = run_forward(
        seq, rep, T, doc_lengths, gate_bias, decay_rate, rows, cotangent, gain_in, in_weight, small_weight, conv_weight, gain
    )
    result, grad_residual, mid_all, grad_gain_mid = run_feed(
        seq, T, rows, gated, cotangent, out_weight, gain_mid, gate_up_weight, down_weight
    )
    parts = run_back(
        seq, stream, rep, T, doc_lengths, gate_bias, decay_rate, rows, grad_residual, gain_in, grad_gain_mid, small_weight,
        conv_weight, gain, mid_all, out_all, gate_up_weight, down_weight, out_weight, head_rows, proj, small, mixed, states,
        news, invs, normed, in_weight,
    )
    result, grad_input, g_in, g_out, g_gate_up, g_down, g_gain_in, g_gain_mid, g_small, g_bias, g_rate, g_taps, g_gain_head = (
        run_output(seq, rep, result, *parts)
    )
    return (
        result[None], grad_input[None], g_gain_in.reshape(D), g_in, g_small.T, g_bias, g_rate, g_taps,
        g_gain_head.reshape(HD), g_out, g_gain_mid.reshape(D), g_gate_up, g_down,
    )


def solution(mesh):
    rows, whole, split = P("stream", "seq", None), P(), P(("seq", "stream"), None)
    return jax.shard_map(
        on_device,
        mesh=mesh,
        in_specs=(rows, rows, P("stream", None)) + (whole,) * 11,
        out_specs=(rows, rows, whole, split, whole, whole, whole, whole, whole, split, whole, split, split),
        check_vma=False,
    )
```

profile of v0, /device:TPU:0, one launch (start us, length us, event | category | flops | bytes accessed | tf_op | source)
XLA Modules:
  0.0 165.2 jit_solution(12884814576839747949)
XLA Ops:
  0.6 44.1 %mixer_forward.1 = (bf16[128,1024]{1,0:T(8,128)(2,1)}, bf16[1024,1024]{1,0:T(8,128)(2,1)}, bf16[1024,1024]{1,0:T(8,128)(2,1)}, bf16[1024,768]{1,0:T(8,128)(2,1)}...) custom-call(s32[1,8]{1,0:T(1,128)} %lengths.3, ...), custom_call_target="tpu_custom_call" | custom-call | tf_op jit(solution)/shard_map/mixer_forward/pallas_call | solution.py:540
  44.7 22.3 %feed_forward.1 = (bf16[128,1024]{1,0:T(8,128)(2,1)}, f32[128,1024]{1,0:T(8,128)}, bf16[1024,1024]{1,0:T(8,128)(2,1)}, f32[1,1024]{1,0:T(1,128)}) custom-call(bf16[128,1024]{1,0:T(8,128)(2,1)} %bitcast.13, bf16[128,1024]{1,0:T(8,128)(2,1)} %get-tuple-element.46.gated, bf16[128,1024]{1,0:T(8,128)(2,1)} %bitcast.16, bf16[1024,1024]{1,0:T(8,128)(2,1)} %w_out.3, ...), custom_call_target="tpu_custom_call" | custom-call | tf_op jit(solution)/shard_map/feed_forward/pallas_call | solution.py:615
  67.0 94.7 %backward.1 = (f32[128,1024]{1,0:T(8,128)}, bf16[8,32,768]{2,1,0:T(8,128)(2,1)}, f32[32,1024]{1,0:T(8,128)}, bf16[8,2,32,352]{3,2,1,0:T(8,128)(2,1)}, f32[88,1024]{1,0:T(8,128)}, /*index=5*/f32[8,8,1024]{2,1,0:T(8,128)}) custom-call(s32[1,8]{1,0:T(1,128)} %lengths.3, f32[8]{0:T(128)} %bias_ref.3, f32[8]{0:T(128)} %rate_ref.3, bf16[128,1024]{1,0:T(8,128)(2,1)} %bitcast.14, ...), custom_call_target="tpu_custom_call" | custom-call | tf_op jit(solution)/shard_map/backward/pallas_call | solution.py:1200
  161.7 3.3 %outputs.1 = (bf16[128,1024]{1,0:T(8,128)(2,1)}, f32[128,1024]{1,0:T(8,128)}, f32[32,6144]{1,0:T(8,128)}, f32[32,1024]{1,0:T(8,128)}, f32[32,5632]{1,0:T(8,128)}...) custom-call(bf16[128,1024]{1,0:T(8,128)(2,1)} %get-tuple-element.47., ...), custom_call_target="tpu_custom_call" | custom-call | tf_op jit(solution)/shard_map/outputs/pallas_call | solution.py:1266
where the time goes:
time: 166 us; the launch traced here: 165 us
  Pallas kernels  164 us (99%)
    pallas_call x1, Pallas kernels, run_back(): pl.pallas_call(functools.partial(back_kernel, n, m, rep, T, piece, shard,...  94.7 us
    pallas_call x1, Pallas kernels, run_forward(): pl.pallas_call(functools.partial(forward_kernel, n, rep, T), out_shape=(s...  44.1 us
    pallas_call x1, Pallas kernels, run_feed(): pl.pallas_call(functools.partial(feed_kernel, n, T, steps), grid=(steps,)...  22.3 us
    pallas_call x1, Pallas kernels, run_output(): pl.pallas_call(functools.partial(output_kernel, n, rep, shard), out_shape...  3.33 us

commit v1 on v0

--- a/solution.py
+++ b/solution.py
@@ -1034,7 +1034,7 @@
 
         for i, (chain, q) in enumerate(hops):
 
-            @pl.when(k == 3 * i // 2)
+            @pl.when(k == 4 * i // 3)
             def _():
                 chain.tick(q)
 
@@ -1108,7 +1108,7 @@
         join(0)
     ins = [line(i) for i in range(lines)]
     for i, (chain, q) in enumerate(hops):
-        if 3 * i // 2 >= n:
+        if 4 * i // 3 >= n:
             chain.tick(q)
 
     def write_down(x):

time: 166 us -> 163 us (0.982)
  Pallas kernels: 164 us -> 161 us
    pallas_call x1, Pallas kernels: 94.7 us -> 91.8 us  [run_back(): pl.pallas_call(functools.partial(back_kernel, n, m, rep, T, piece, shard,...]
where the time goes in v1:
time: 163 us; the launch traced here: 162 us
  Pallas kernels  161 us (99%)
    pallas_call x1, Pallas kernels, run_back(): pl.pallas_call(functools.partial(back_kernel, n, m, rep, T, piece, shard,...  91.8 us
    pallas_call x1, Pallas kernels, run_forward(): pl.pallas_call(functools.partial(forward_kernel, n, rep, T), out_shape=(s...  44.1 us
    pallas_call x1, Pallas kernels, run_feed(): pl.pallas_call(functools.partial(feed_kernel, n, T, steps), grid=(steps,)...  22.3 us
    pallas_call x1, Pallas kernels, run_output(): pl.pallas_call(functools.partial(output_kernel, n, rep, shard), out_shape...  3.33 us

profile of v1, /device:TPU:0, one launch (start us, length us, event | category | flops | bytes accessed | tf_op | source)
XLA Modules:
  0.0 162.3 jit_solution(726751303896751628)
XLA Ops:
  0.6 44.1 %mixer_forward.1 = (bf16[128,1024]{1,0:T(8,128)(2,1)}, bf16[1024,1024]{1,0:T(8,128)(2,1)}, bf16[1024,1024]{1,0:T(8,128)(2,1)}, bf16[1024,768]{1,0:T(8,128)(2,1)}...) custom-call(s32[1,8]{1,0:T(1,128)} %lengths.3, ...), custom_call_target="tpu_custom_call" | custom-call | tf_op jit(solution)/shard_map/mixer_forward/pallas_call | solution.py:540
  44.7 22.3 %feed_forward.1 = (bf16[128,1024]{1,0:T(8,128)(2,1)}, f32[128,1024]{1,0:T(8,128)}, bf16[1024,1024]{1,0:T(8,128)(2,1)}, f32[1,1024]{1,0:T(1,128)}) custom-call(bf16[128,1024]{1,0:T(8,128)(2,1)} %bitcast.13, bf16[128,1024]{1,0:T(8,128)(2,1)} %get-tuple-element.46.gated, bf16[128,1024]{1,0:T(8,128)(2,1)} %bitcast.16, bf16[1024,1024]{1,0:T(8,128)(2,1)} %w_out.3, ...), custom_call_target="tpu_custom_call" | custom-call | tf_op jit(solution)/shard_map/feed_forward/pallas_call | solution.py:615
  67.0 91.8 %backward.1 = (f32[128,1024]{1,0:T(8,128)}, bf16[8,32,768]{2,1,0:T(8,128)(2,1)}, f32[32,1024]{1,0:T(8,128)}, bf16[8,2,32,352]{3,2,1,0:T(8,128)(2,1)}, f32[88,1024]{1,0:T(8,128)}, /*index=5*/f32[8,8,1024]{2,1,0:T(8,128)}) custom-call(s32[1,8]{1,0:T(1,128)} %lengths.3, f32[8]{0:T(128)} %bias_ref.3, f32[8]{0:T(128)} %rate_ref.3, bf16[128,1024]{1,0:T(8,128)(2,1)} %bitcast.14, ...), custom_call_target="tpu_custom_call" | custom-call | tf_op jit(solution)/shard_map/backward/pallas_call | solution.py:1200
  158.8 3.3 %outputs.1 = (bf16[128,1024]{1,0:T(8,128)(2,1)}, f32[128,1024]{1,0:T(8,128)}, f32[32,6144]{1,0:T(8,128)}, f32[32,1024]{1,0:T(8,128)}, f32[32,5632]{1,0:T(8,128)}...) custom-call(bf16[128,1024]{1,0:T(8,128)(2,1)} %get-tuple-element.47., ...), custom_call_target="tpu_custom_call" | custom-call | tf_op jit(solution)/shard_map/outputs/pallas_call | solution.py:1266

commit v2 on v1

--- a/solution.py
+++ b/solution.py
@@ -1019,7 +1019,7 @@
         def _():
             owner_copy(j).start()
 
-    hops = [(chain, q) for chain in (downs, *ups) for q in range(1, m - 1)]
+    hops = [(chain, q) for chain in (downs, *ups, outs) for q in range(1, m - 1)]
 
     def after_turn(k):
         c = n - 1 - k
@@ -1034,7 +1034,7 @@
 
         for i, (chain, q) in enumerate(hops):
 
-            @pl.when(k == 4 * i // 3)
+            @pl.when(k == i)
             def _():
                 chain.tick(q)
 
@@ -1108,7 +1108,7 @@
         join(0)
     ins = [line(i) for i in range(lines)]
     for i, (chain, q) in enumerate(hops):
-        if 4 * i // 3 >= n:
+        if i >= n:
             chain.tick(q)
 
     def write_down(x):
@@ -1128,8 +1128,6 @@
     for copy in q_ups:
         copy.start()
     q_gu_in[me] = q_gu[me]
-    for q in range(1, m - 1):
-        outs.tick(q)
 
     def input_gradient():
         total = part_own[chip].astype(f32)

time: 163 us -> 162 us (level)
  no operation moved by 1% of the time
where the time goes in v2:
time: 162 us; the launch traced here: 161 us
  Pallas kernels  161 us (99%)
    pallas_call x1, Pallas kernels, run_back(): pl.pallas_call(functools.partial(back_kernel, n, m, rep, T, piece, shard,...  90.9 us
    pallas_call x1, Pallas kernels, run_forward(): pl.pallas_call(functools.partial(forward_kernel, n, rep, T), out_shape=(s...  44.1 us
    pallas_call x1, Pallas kernels, run_feed(): pl.pallas_call(functools.partial(feed_kernel, n, T, steps), grid=(steps,)...  22.3 us
    pallas_call x1, Pallas kernels, run_output(): pl.pallas_call(functools.partial(output_kernel, n, rep, shard), out_shape...  3.33 us

profile of v2, /device:TPU:0, one launch (start us, length us, event | category | flops | bytes accessed | tf_op | source)
XLA Modules:
  0.0 161.5 jit_solution(8977017391238066392)
XLA Ops:
  0.6 44.1 %mixer_forward.1 = (bf16[128,1024]{1,0:T(8,128)(2,1)}, bf16[1024,1024]{1,0:T(8,128)(2,1)}, bf16[1024,1024]{1,0:T(8,128)(2,1)}, bf16[1024,768]{1,0:T(8,128)(2,1)}...) custom-call(s32[1,8]{1,0:T(1,128)} %lengths.3, ...), custom_call_target="tpu_custom_call" | custom-call | tf_op jit(solution)/shard_map/mixer_forward/pallas_call | solution.py:540
  44.7 22.3 %feed_forward.1 = (bf16[128,1024]{1,0:T(8,128)(2,1)}, f32[128,1024]{1,0:T(8,128)}, bf16[1024,1024]{1,0:T(8,128)(2,1)}, f32[1,1024]{1,0:T(1,128)}) custom-call(bf16[128,1024]{1,0:T(8,128)(2,1)} %bitcast.13, bf16[128,1024]{1,0:T(8,128)(2,1)} %get-tuple-element.46.gated, bf16[128,1024]{1,0:T(8,128)(2,1)} %bitcast.16, bf16[1024,1024]{1,0:T(8,128)(2,1)} %w_out.3, ...), custom_call_target="tpu_custom_call" | custom-call | tf_op jit(solution)/shard_map/feed_forward/pallas_call | solution.py:615
  67.0 90.9 %backward.1 = (f32[128,1024]{1,0:T(8,128)}, bf16[8,32,768]{2,1,0:T(8,128)(2,1)}, f32[32,1024]{1,0:T(8,128)}, bf16[8,2,32,352]{3,2,1,0:T(8,128)(2,1)}, f32[88,1024]{1,0:T(8,128)}, /*index=5*/f32[8,8,1024]{2,1,0:T(8,128)}) custom-call(s32[1,8]{1,0:T(1,128)} %lengths.3, f32[8]{0:T(128)} %bias_ref.3, f32[8]{0:T(128)} %rate_ref.3, bf16[128,1024]{1,0:T(8,128)(2,1)} %bitcast.14, ...), custom_call_target="tpu_custom_call" | custom-call | tf_op jit(solution)/shard_map/backward/pallas_call | solution.py:1198
  158.0 3.3 %outputs.1 = (bf16[128,1024]{1,0:T(8,128)(2,1)}, f32[128,1024]{1,0:T(8,128)}, f32[32,6144]{1,0:T(8,128)}, f32[32,1024]{1,0:T(8,128)}, f32[32,5632]{1,0:T(8,128)}...) custom-call(bf16[128,1024]{1,0:T(8,128)(2,1)} %get-tuple-element.47., ...), custom_call_target="tpu_custom_call" | custom-call | tf_op jit(solution)/shard_map/outputs/pallas_call | solution.py:1264
